TPU v7x, 256 devices: a whole 4x4x8 slice. The times are simulated.
256 devices in a mesh: srow: 8 (over z_lo, y), scol: 8 (over x, core), hour: 4 (over z_hi).
Axes of the slice: x: 4, y: 4, z: 8 (z_hi: 4, z_lo: 2; z = z_hi * 2 + z_lo), core: 2. Of those that a mesh axis runs over, the one named last changes fastest.
Arguments:
- readings: bfloat16 [32768, 4608], P(('srow', 'scol'), 'hour'), may hold values from -18 to 18
- space_basis: bfloat16 [32768, 32768], P('srow', ('scol', 'hour')), may hold values from -0.0625 to 0.0625
- time_modes: bfloat16 [4608, 512], P('hour'), may hold values from -0.09375 to 0.09375
- space_power: float32 [32768], P(('scol', 'hour')), may hold values from 0.05 to 20
- time_power: float32 [512], replicated, may hold values from 0.05 to 20
Outputs:
- posterior: bfloat16 [32768, 4608], P(('srow', 'scol'), 'hour')
All inputs are finite; a program needn't handle non-finite values.
Results may differ from a plain program's by a relative error of at most 0.0065.
Values may be sent and summed in bfloat16 or wider, within the bound.
A program may use at most 64 MiB of HBM per device.

v0:
```python
import jax
import jax.numpy as jnp
from jax import lax
from jax.sharding import PartitionSpec as P

noise_level = 1.0


def cut_along(value, dim, peers):
    lengths = value.shape
    blocks = value.reshape(*lengths[:dim], peers, lengths[dim] // peers, *lengths[dim + 1 :])
    return jnp.moveaxis(blocks, dim, 0)


def summed_on_arrival(value, axis, dim):
    blocks = cut_along(value, dim, lax.axis_size(axis))
    arrived = lax.all_to_all(blocks, axis, split_axis=0, concat_axis=0, tiled=True)
    return arrived.sum(axis=0)


def copy_for_each(value, axis):
    copies = jnp.broadcast_to(value, (lax.axis_size(axis), *value.shape))
    return lax.all_to_all(copies, axis, split_axis=0, concat_axis=0, tiled=True)


def joined_along(blocks, dim):
    lengths = list(blocks.shape[1:])
    lengths[dim] *= blocks.shape[0]
    return jnp.moveaxis(blocks, 0, dim).reshape(lengths)


def gather_directly(value, axis, dim):
    blocks = copy_for_each(value, axis)
    return joined_along(blocks, dim)


def on_device(readings, space_basis, time_modes, space_power, time_power):
    coefficients = summed_on_arrival(
        lax.dot_general(
            time_modes, readings, (((0,), (1,)), ((), ())), preferred_element_type=jnp.float32
        ),
        "hour",
        0,
    ).astype(jnp.bfloat16)
    coefficients = gather_directly(coefficients, "scol", 1)
    coefficients = lax.all_gather(coefficients, "hour", axis=0, tiled=True)
    spectral_rows = space_basis.shape[1] // lax.axis_size("srow")
    basis_panel = space_basis
    spectral = summed_on_arrival(
        lax.dot_general(
            basis_panel, coefficients, (((0,), (1,)), ((), ())), preferred_element_type=jnp.float32
        ),
        "srow",
        0,
    )
    spatial_power = lax.dynamic_slice_in_dim(
        space_power, lax.axis_index("srow") * spectral_rows, spectral_rows, 0
    )
    product = spatial_power[:, None] * time_power[None, :]
    scaled = (spectral * (product / (product + noise_level))).astype(jnp.bfloat16)
    scaled = gather_directly(scaled, "srow", 0)
    basis_panel = space_basis
    synthesis = lax.psum_scatter(
        jnp.dot(basis_panel, scaled, preferred_element_type=jnp.float32),
        ("scol", "hour"),
        scatter_dimension=0,
        tiled=True,
    ).astype(jnp.bfloat16)
    synthesis = gather_directly(synthesis, "hour", 0)
    posterior = lax.dot_general(
        synthesis, time_modes, (((1,), (1,)), ((), ())), preferred_element_type=jnp.float32
    )
    return posterior.astype(jnp.bfloat16)


def solution(mesh):
    return jax.shard_map(
        on_device,
        mesh=mesh,
        in_specs=(
            P(("srow", "scol"), "hour"),
            P("srow", ("scol", "hour")),
            P("hour", None),
            P(("scol", "hour")),
            P(),
        ),
        out_specs=P(("srow", "scol"), "hour"),
        check_vma=False,
    )
```

profile of v0, /device:TPU:9, one launch (start us, length us, event | category | flops | bytes accessed | tf_op | source)
XLA Modules:
  0.0 368.3 jit_solution(12886480785887110373)
XLA Ops:
  6.5 0.0 copy-start
  6.5 0.0 all-gather.2.cloned.1.call-start
  6.5 1.3 copy-done
  7.8 2.2 fusion.2
  10.0 33.2 %all_to_all.25 = f32[4,128,512]{2,1,0:T(8,128)S(1)} all-to-all(f32[4,128,512]{2,1,0:T(8,128)S(1)} %bitcast.25), channel_id=1, replica_groups=mesh['srow'=8,'scol'=8,'hour'=4] {'hour'}, dimensions={0} | all-to-all | bytes 2097152 | tf_op jit(solution)/shard_map/all_to_all | solution.py:17
  43.2 0.1 reduce_sum.18
  43.3 0.1 copy.8
  43.4 0.1 broadcast_in_dim.11
  43.6 22.8 %all_to_all.26 = bf16[8,128,512]{1,2,0:T(8,128)(2,1)} all-to-all(bf16[8,128,512]{1,2,0:T(8,128)(2,1)S(1)} %broadcast_in_dim.11), channel_id=1, replica_groups=mesh['srow'=8,'scol'=8,'hour'=4] {'scol'}, dimensions={0} | all-to-all | bytes 2097152 | tf_op jit(solution)/shard_map/all_to_all | solution.py:23
  66.4 0.0 all-gather.2.cloned.1.call-update
  66.4 85.9 %all-gather.2.cloned.1.call-done = bf16[512,4096]{0,1:T(8,128)(2,1)} async-done(((bf16[128,4096]{0,1:T(8,128)(2,1)}), bf16[512,4096]{0,1:T(8,128)(2,1)}) %all-gather.2.cloned.1.call-update) | async-done | bytes 4194320 | tf_op jit(solution)/shard_map/all_gather | solution.py:46
  152.4 8.2 %convolution_bitcast_fusion.1 = f32[64,8,8,128]{3,2,1,0:T(8,128)S(1)} fusion(bf16[512,4096]{0,1:T(8,128)(2,1)} %all-gather.2.cloned.1.call-done, bf16[4096,1024]{1,0:T(8,128)(2,1)} %param.6), kind=kOutput, calls=%fused_computation.3 | convolution fusion | flops 4294967296 | bytes 14680064 | tf_op jit(solution)/shard_map/dot_general | solution.py:50
  160.6 1.5 copy.16
  162.1 4.3 %all-to-all-start.2 = ((f32[8,128,512]{1,2,0:T(8,128)}), f32[8,128,512]{1,2,0:T(8,128)S(1)}, u32[]{:S(2)}, u32[]{:S(2)}) async-start(f32[8,128,512]{1,2,0:T(8,128)} %bitcast.22), calls=%async_computation.2 | async-start | bytes 4194304 | tf_op jit(solution)/shard_map/all_to_all | solution.py:17
  166.3 0.0 copy-start.1
  166.3 0.0 reduce-scatter.2.cloned.1.call-start
  166.3 0.8 dynamic_slice.3
  167.1 23.9 %all-to-all-done.2 = f32[8,128,512]{1,2,0:T(8,128)S(1)} async-done(((f32[8,128,512]{1,2,0:T(8,128)}), f32[8,128,512]{1,2,0:T(8,128)S(1)}, u32[]{:S(2)}, u32[]{:S(2)}) %all-to-all-start.2) | async-done | bytes 2097184 | tf_op jit(solution)/shard_map/all_to_all | solution.py:17
  191.0 0.1 reduce_sum.19
  191.1 0.0 copy-done.1
  191.2 0.1 fusion.1
  191.3 0.1 copy.11
  191.4 0.1 broadcast_in_dim.12
  191.5 17.7 %all_to_all.27 = bf16[8,128,512]{2,1,0:T(8,128)(2,1)S(1)} all-to-all(bf16[8,128,512]{2,1,0:T(8,128)(2,1)S(1)} %broadcast_in_dim.12), channel_id=1, replica_groups=mesh['srow'=8,'scol'=8,'hour'=4] {'srow'}, dimensions={0} | all-to-all | bytes 2097152 | tf_op jit(solution)/shard_map/all_to_all | solution.py:23
  209.2 10.3 %convolution_bitcast_fusion = f32[4096,512]{0,1:T(8,128)} fusion(bf16[1024,512]{1,0:T(8,128)(2,1)S(1)} %bitcast.24, bf16[4096,1024]{1,0:T(8,128)(2,1)} %param.6), kind=kOutput, calls=%fused_computation | convolution fusion | flops 4294967296 | bytes 17825792 | tf_op jit(solution)/shard_map/dot_general | solution.py:64
  219.5 0.0 reduce-scatter.2.cloned.1.call-update
  219.5 120.7 %reduce-scatter.2.cloned.1.call-done = f32[128,512]{0,1:T(8,128)} async-done(((f32[4096,512]{0,1:T(8,128)}), f32[128,512]{0,1:T(8,128)}) %reduce-scatter.2.cloned.1.call-update) | async-done | bytes 262160 | tf_op jit(solution)/shard_map/reduce_scatter | solution.py:63
  340.2 1.0 convert_element_type.14
  341.2 0.1 copy.12
  341.4 18.2 %all_to_all.28 = bf16[4,128,512]{2,1,0:T(8,128)(2,1)S(1)} all-to-all(bf16[4,128,512]{2,1,0:T(8,128)(2,1)S(1)} %broadcast_in_dim.13), channel_id=1, replica_groups=mesh['srow'=8,'scol'=8,'hour'=4] {'hour'}, dimensions={0} | all-to-all | bytes 1048576 | tf_op jit(solution)/shard_map/all_to_all | solution.py:23
  359.6 1.9 convolution_convert_fusion
  (1 shorter events, 0.0 us)
Async XLA Ops:
  6.5 1.3 copy-start
  6.5 145.9 %all-gather.2.cloned.1.call-start = ((), (), s32[]{:S(2)}) async-start(), calls=%async_computation.6 | async-start | bytes 5242880 | tf_op jit(solution)/shard_map/all_gather | solution.py:46
  162.1 28.9 %all-to-all-start.2 = ((f32[8,128,512]{1,2,0:T(8,128)}), f32[8,128,512]{1,2,0:T(8,128)S(1)}, u32[]{:S(2)}, u32[]{:S(2)}) async-start(f32[8,128,512]{1,2,0:T(8,128)} %bitcast.22), calls=%async_computation.2 | async-start | bytes 4194304 | tf_op jit(solution)/shard_map/all_to_all | solution.py:17
  166.3 24.8 %copy-start.1 = (f32[512]{0:T(512)S(1)}, f32[512]{0:T(512)}, u32[]{:S(2)}) copy-start(f32[512]{0:T(512)} %param.9) | copy-start | bytes 6148
  166.3 173.9 %reduce-scatter.2.cloned.1.call-start = ((), (), s32[]{:S(2)}) async-start(), calls=%async_computation.7 | async-start | bytes 8650752 | tf_op jit(solution)/shard_map/reduce_scatter | solution.py:63
Sparse Core Ops, SparseCore 0:
  66.6 85.7 all-gather.1
  219.6 120.5 reduce-scatter.1
where the time goes:
time: 371 us; the launch traced here: 368 us
  waiting for transfers between devices  231 us (62%)
  blocking collectives  92 us (25%)
  matrix products  22.5 us (6%)
  between operations  13.5 us (4%)
  starting transfers between devices  4.27 us (1%)
  local copies, waits for them, and re-layouts  4.12 us (1%)
    reduce_scatter x1, waiting for transfers between devices, on_device(): lax.psum_scatter(jnp.dot(basis_panel, scaled, preferred_element_type=jnp....  121 us
    all_gather x1, waiting for transfers between devices, on_device(): coefficients = lax.all_gather(coefficients, 'hour', axis=0, tiled=True)  85.9 us
    all_to_all x3, blocking collectives, copy_for_each(): return lax.all_to_all(copies, axis, split_axis=0, concat_axis=0, tiled=True)  58.7 us
    all_to_all x1, blocking collectives, summed_on_arrival(): lax.all_to_all(blocks, axis, split_axis=0, concat_axis=0, tiled=True)  33.2 us
    all_to_all x1, waiting for transfers between devices, summed_on_arrival(): lax.all_to_all(blocks, axis, split_axis=0, concat_axis=0, tiled=True)  23.9 us
    dot_general x1, matrix products, on_device(): jnp.dot(basis_panel, scaled, preferred_element_type=jnp.float32)  10.3 us
    dot_general x1, matrix products, on_device(): lax.dot_general(basis_panel, coefficients, (((0,), (1,)), ((), ())), pref...  8.21 us
  transfers between devices with their start and end apart: 3, of which 3 were waited for; matrix products, arithmetic and copies ran while one was open for 0% of the time, Pallas kernels for 0%

commit v1 on v0

v1 whole, which is shorter than its diff:
```python
import functools

import jax
import jax.numpy as jnp
from jax import lax
from jax.experimental import pallas as pl
from jax.experimental.pallas import tpu as pltpu
from jax.sharding import PartitionSpec as P

MESH = pl.DeviceIdType.MESH
F32, BF16 = jnp.float32, jnp.bfloat16
noise_level = 1.0

CHUNKS = 4
SPACING = 1
X, Y, HOURS = 4, 4, 4

COPIES = dict(hour_sum=3, hour_gather=3, x_gather=3, core_gather=4, y_sum=3, z_sum=1, y_gather=3, core_sum=4, x_sum=3, last_sum=3, last_gather=3)
FIRST = {}
for _name, _count in COPIES.items():
    FIRST[_name] = sum(COPIES[n] for n in FIRST)
TOTAL_COPIES = sum(COPIES.values())


def kernel(
    r_ref, t_ref, b_hbm, space_ref, time_ref, out_ref,
    b, part, part_out, part_in, coef, y_own, y_out, y_in, z_out, z_in, scaled,
    core_out, core_in, own, x_out, x_in, h_own, h_out, h_in, syn,
    send_sem, recv_sem, b_sem,
):
    srow, scol, hour = lax.axis_index("srow"), lax.axis_index("scol"), lax.axis_index("hour")
    low, y = srow // Y, srow % Y
    x, core = scol // 2, scol % 2
    modes = part.shape[2]
    width = b.shape[2]
    sites = r_ref.shape[0]

    def hour_peer(o):
        return (srow, scol, (hour + o) % HOURS)

    def x_peer(o):
        return (srow, ((x + o) % X) * 2 + core, hour)

    def y_peer(o):
        return (low * Y + (y + o) % Y, scol, hour)

    core_peer = (srow, x * 2 + (1 - core), hour)
    low_peer = ((1 - low) * Y + y, scol, hour)

    started = {}

    def send(name, i, q, src, dst, peer):
        at = FIRST[name] + i
        copy = pltpu.make_async_remote_copy(
            src_ref=src, dst_ref=dst, send_sem=send_sem.at[q, at], recv_sem=recv_sem.at[q, at],
            device_id=peer, device_id_type=MESH,
        )
        copy.start()
        started[name, i, q] = copy

    def arrived(name, i, q):
        started[name, i, q].wait_recv()

    def group(c):
        return pl.ds(pl.multiple_of(c * sites, sites), sites)

    barrier = pltpu.get_barrier_semaphore()
    peers = [f(o) for f in (hour_peer, x_peer, y_peer) for o in (1, 2, 3)] + [core_peer, low_peer]
    for peer in peers:
        pl.semaphore_signal(barrier, inc=1, device_id=peer, device_id_type=MESH)
    for j in range(b.shape[0]):
        pltpu.make_async_copy(b_hbm.at[:, pl.ds(j * width, width)], b.at[j], b_sem.at[j]).start()

    def project(q):
        value = lax.dot_general(
            t_ref[:, q * modes : (q + 1) * modes], r_ref[...], (((0,), (1,)), ((), ())), preferred_element_type=F32
        )
        for i in range(HOURS):
            block = value[:, i * modes_sites : (i + 1) * modes_sites]
            part[q, i] = block
            part_out[q, i] = block.astype(BF16)
        if q == 0:
            pl.semaphore_wait(barrier, len(peers))
        for o in (2, 1, 3):
            send("hour_sum", o - 1, q, part_out.at[q, (hour + o) % HOURS], part_in.at[q, o - 1], hour_peer(o))

    modes_sites = part.shape[3]

    def sum_hours(q):
        total = part[q, hour]
        for o in (1, 3, 2):
            arrived("hour_sum", o - 1, q)
            total += part_in[q, o - 1].astype(F32)
        mine = scol * HOURS + hour
        coef[q, mine] = total.astype(BF16)
        for o in (2, 1, 3):
            send("hour_gather", o - 1, q, coef.at[q, mine], coef.at[q, mine], hour_peer(o))

    def gather_x(q):
        for o in (1, 3, 2):
            arrived("hour_gather", o - 1, q)
        mine = coef.at[q, pl.ds(scol * HOURS, HOURS)]
        for o in (2, 1, 3):
            send("x_gather", o - 1, q, mine, mine, x_peer(o))
        send("core_gather", 0, q, mine, mine, core_peer)

    def half(q, j, of_core):
        total = None
        for i in range(X):
            c = i * 2 + of_core
            left = jnp.concatenate([coef[q, c * HOURS + n] for n in range(HOURS)], axis=1)
            term = jnp.dot(left, b[j, group(c), :], preferred_element_type=F32)
            total = term if total is None else total + term
        return total

    def analyse(q):
        for o in (1, 3, 2):
            arrived("x_gather", o - 1, q)
            c = ((x + X - o) % X) * 2 + core
            other = coef.at[q, pl.ds(c * HOURS, HOURS)]
            send("core_gather", o, q, other, other, core_peer)
        if q == 0:
            for j in range(b.shape[0]):
                pltpu.make_async_copy(b_hbm.at[:, pl.ds(j * width, width)], b.at[j], b_sem.at[j]).wait()

        def first(j, carry):
            y_own[q, j] = half(q, j, core)
            return carry

        lax.fori_loop(0, Y, first, 0)
        for i in range(4):
            arrived("core_gather", i, q)

        def second(j, carry):
            total = y_own[q, j] + half(q, j, 1 - core)
            y_own[q, j] = total
            y_out[q, j] = total.astype(BF16)
            return carry

        lax.fori_loop(0, Y, second, 0)
        for o in (2, 1, 3):
            send("y_sum", o - 1, q, y_out.at[q, (y + o) % Y], y_in.at[q, o - 1], y_peer(o))

    def sum_y(q):
        total = y_own[q, y]
        for o in (1, 3, 2):
            arrived("y_sum", o - 1, q)
            total += y_in[q, o - 1].astype(F32)
        y_own[q, y] = total
        z_out[q] = total.astype(BF16)
        send("z_sum", 0, q, z_out.at[q], z_in.at[q], low_peer)

    def scale(q):
        arrived("z_sum", 0, q)
        total = y_own[q, y] + z_in[q].astype(F32)
        product = time_ref[q * modes : (q + 1) * modes, :] * space_ref[y]
        scaled[q, y] = (total * (product / (product + noise_level))).astype(BF16)
        for o in (2, 1, 3):
            send("y_gather", o - 1, q, scaled.at[q, y], scaled.at[q, y], y_peer(o))

    def synthesise(q):
        for o in (1, 3, 2):
            arrived("y_gather", o - 1, q)

        def term(c):
            total = None
            for j in range(Y):
                one = lax.dot_general(
                    scaled[q, j], b[j, group(c), :], (((1,), (1,)), ((), ())), preferred_element_type=F32
                )
                total = one if total is None else total + one
            return total

        for o in (2, 1, 3, 0):
            to = (x + o) % X
            core_out[q, to] = term(to * 2 + (1 - core))
            send("core_sum", o, q, core_out.at[q, to], core_in.at[q, to], core_peer)
        for o in (2, 1, 3, 0):
            to = (x + o) % X
            value = term(to * 2 + core)
            arrived("core_sum", o, q)
            value += core_in[q, to]
            if o:
                x_out[q, to] = value.astype(BF16)
                send("x_sum", o - 1, q, x_out.at[q, to], x_in.at[q, o - 1], x_peer(o))
            else:
                own[q] = value

    def sum_x(q):
        total = own[q]
        for o in (1, 3, 2):
            arrived("x_sum", o - 1, q)
            total += x_in[q, o - 1].astype(F32)
        for i in range(HOURS):
            block = total[:, i * modes_sites : (i + 1) * modes_sites]
            h_own[q, i] = block
            h_out[q, i] = block.astype(BF16)
        for o in (2, 1, 3):
            send("last_sum", o - 1, q, h_out.at[q, (hour + o) % HOURS], h_in.at[q, o - 1], hour_peer(o))

    def sum_last(q):
        total = h_own[q, hour]
        for o in (1, 3, 2):
            arrived("last_sum", o - 1, q)
            total += h_in[q, o - 1].astype(F32)
        mine = syn.at[hour, pl.ds(q * modes, modes)]
        mine[...] = total.astype(BF16)
        for o in (2, 1, 3):
            send("last_gather", o - 1, q, mine, mine, hour_peer(o))

    def finish(q):
        for o in (1, 3, 2):
            arrived("last_gather", o - 1, q)

    stages = [project, sum_hours, gather_x, analyse, sum_y, scale, synthesise, sum_x, sum_last, finish]
    for step in range(len(stages) + SPACING * (CHUNKS - 1)):
        for q in range(CHUNKS):
            at = step - SPACING * q
            if 0 <= at < len(stages):
                stages[at](q)

    def posterior(i, carry):
        value = lax.dot_general(syn[i], t_ref[...], (((0,), (1,)), ((), ())), preferred_element_type=F32)
        out_ref[pl.ds(pl.multiple_of(i * modes_sites, modes_sites), modes_sites), :] = value.astype(out_ref.dtype)
        return carry

    lax.fori_loop(0, HOURS, posterior, 0)
    for copy in started.values():
        copy.wait_send()


def on_device(readings, space_basis, time_modes, space_power, time_power):
    sites, hours = readings.shape
    rows, columns = space_basis.shape
    every_mode = time_modes.shape[1]
    modes, piece, width = every_mode // CHUNKS, sites // HOURS, columns // Y
    groups = rows // sites

    def chunked(dtype, *shape):
        return pltpu.VMEM((CHUNKS, *shape), dtype)

    in_vmem = pl.BlockSpec(memory_space=pltpu.VMEM)
    return pl.pallas_call(
        kernel,
        out_shape=jax.ShapeDtypeStruct((sites, hours), BF16),
        in_specs=[in_vmem, in_vmem, pl.BlockSpec(memory_space=pl.ANY), in_vmem, in_vmem],
        out_specs=in_vmem,
        scratch_shapes=[
            pltpu.VMEM((Y, rows, width), BF16),
            chunked(F32, HOURS, modes, piece),
            chunked(BF16, HOURS, modes, piece),
            chunked(BF16, 3, modes, piece),
            chunked(BF16, groups * HOURS, modes, piece),
            chunked(F32, Y, modes, width),
            chunked(BF16, Y, modes, width),
            chunked(BF16, 3, modes, width),
            chunked(BF16, modes, width),
            chunked(BF16, modes, width),
            chunked(BF16, Y, modes, width),
            chunked(F32, X, modes, sites),
            chunked(F32, X, modes, sites),
            chunked(F32, modes, sites),
            chunked(BF16, X, modes, sites),
            chunked(BF16, 3, modes, sites),
            chunked(F32, HOURS, modes, piece),
            chunked(BF16, HOURS, modes, piece),
            chunked(BF16, 3, modes, piece),
            pltpu.VMEM((HOURS, every_mode, piece), BF16),
            pltpu.SemaphoreType.DMA((CHUNKS, TOTAL_COPIES)),
            pltpu.SemaphoreType.DMA((CHUNKS, TOTAL_COPIES)),
            pltpu.SemaphoreType.DMA((Y,)),
        ],
        compiler_params=pltpu.CompilerParams(
            collective_id=0, has_side_effects=True, vmem_limit_bytes=58 * 2**20
        ),
        name="transform",
    )(readings, time_modes, space_basis, space_power.reshape(Y, 1, width), time_power.reshape(every_mode, 1))


def solution(mesh):
    return jax.shard_map(
        on_device,
        mesh=mesh,
        in_specs=(
            P(("srow", "scol"), "hour"),
            P("srow", ("scol", "hour")),
            P("hour", None),
            P(("scol", "hour")),
            P(),
        ),
        out_specs=P(("srow", "scol"), "hour"),
        check_vma=False,
    )
```

time: 371 us -> 118 us (0.32)
  waiting for transfers between devices: 231 us -> 0 us
  Pallas kernels: 0 us -> 113 us
  blocking collectives: 92 us -> 0 us
  matrix products: 22.5 us -> 0 us
  between operations: 13.5 us -> 0.01 us
  starting transfers between devices: 4.27 us -> 0 us
    reduce_scatter x1 -> x0, waiting for transfers between devices: 121 us -> none  [on_device(): lax.psum_scatter(jnp.dot(basis_panel, scaled, preferred_element_type=jnp....]
    pallas_call x0 -> x1, Pallas kernels: none -> 113 us  [on_device(): pl.pallas_call(kernel, out_shape=jax.ShapeDtypeStruct((sites, hours), BF1...]
    all_to_all x4 -> x0, blocking collectives: 92 us -> none  [the longest x3 58.7 us: copy_for_each(): return lax.all_to_all(copies, axis, split_axis=0, concat_axis=0, tiled=True)]
    all_gather x1 -> x0, waiting for transfers between devices: 85.9 us -> none  [on_device(): coefficients = lax.all_gather(coefficients, 'hour', axis=0, tiled=True)]
    all_to_all x1 -> x0, waiting for transfers between devices: 23.9 us -> none  [summed_on_arrival(): lax.all_to_all(blocks, axis, split_axis=0, concat_axis=0, tiled=True)]
    dot_general x4 -> x0, matrix products: 22.5 us -> none  [the longest x1 10.3 us: on_device(): jnp.dot(basis_panel, scaled, preferred_element_type=jnp.float32)]
    all_to_all x1 -> x0, starting transfers between devices: 4.26 us -> none  [summed_on_arrival(): lax.all_to_all(blocks, axis, split_axis=0, concat_axis=0, tiled=True)]
  transfers between devices with their start and end apart: 3 -> 0, of which waited for: 3 -> 0; matrix products, arithmetic and copies ran while one was open for 0% -> 0% of each run, Pallas kernels for 0% -> 0%
where the time goes in v1:
time: 118 us; the launch traced here: 117 us
  Pallas kernels  113 us (96%)
  local copies, waits for them, and re-layouts  3.91 us (3%)
    pallas_call x1, Pallas kernels, on_device(): pl.pallas_call(kernel, out_shape=jax.ShapeDtypeStruct((sites, hours), BF1...  113 us
    unnamed x1, local copies, waits for them, and re-layouts  2.37 us

profile of v1, /device:TPU:9, one launch (start us, length us, event | category | flops | bytes accessed | tf_op | source)
XLA Modules:
  0.0 117.1 jit_solution(15849088105410230780)
XLA Ops:
  0.0 1.5 %copy.6.time_ref = f32[512,1]{1,0:T(8,128)} copy(f32[512,1]{0,1:T(1,128)} %bitcast.3) | data formatting | bytes 4096 | tf_op jit(solution)/shard_map/reshape | solution.py:277
  1.5 113.1 %transform.1 = bf16[512,1152]{1,0:T(8,128)(2,1)} custom-call(bf16[512,1152]{1,0:T(8,128)(2,1)} %r_ref.1, bf16[1152,512]{1,0:T(8,128)(2,1)} %t_ref.1, bf16[4096,1024]{1,0:T(8,128)(2,1)} %b_hbm.1, f32[4,1,256]{2,1,0:T(1,128)} %bitcast.2, f32[512,1]{1,0:T(8,128)} %copy.6.time_ref), custom_call_target="tpu_custom_call" | custom-call | tf_op jit(solution)/shard_map/transform/pallas_call | solution.py:243
  114.7 2.4 %copy.8 = bf16[512,1152]{1,0:T(8,128)(2,1)} copy(bf16[512,1152]{1,0:T(8,128)(2,1)} %transform.1) | data formatting | bytes 2359296

commit v2 on v1

v2 whole, which is shorter than its diff:
```python
import functools

import jax
import jax.numpy as jnp
from jax import lax
from jax.experimental import pallas as pl
from jax.experimental.pallas import tpu as pltpu
from jax.sharding import PartitionSpec as P

MESH = pl.DeviceIdType.MESH
F32, BF16 = jnp.float32, jnp.bfloat16
noise_level = 1.0

SLICES = ((0, 128), (128, 128), (256, 128), (384, 128))
CHUNKS = len(SLICES)
LANES = 128
X, Y, HOURS = 4, 4, 4

ORDER = (
    (0, 3), (0, 0), (0, 1), (1, 3), (1, 1), (0, 2), (2, 3), (1, 2), (2, 1), (3, 3), (2, 2), (1, 0), (3, 1), (4, 3),
    (2, 0), (5, 3), (4, 1), (3, 2), (5, 1), (6, 3), (3, 0), (4, 2), (6, 1), (5, 2), (4, 0), (7, 3), (5, 0), (6, 2),
    (7, 1), (6, 0), (8, 3), (8, 1), (7, 2), (7, 0), (8, 2), (8, 0), (9, 3), (9, 1), (9, 0), (9, 2),
)

COPIES = dict(hour_sum=3, hour_gather=3, x_gather=3, core_gather=4, y_sum=3, z_sum=1, y_gather=3, core_sum=4, x_sum=3, last_sum=3, last_gather=3)
FIRST = {}
for _name, _count in COPIES.items():
    FIRST[_name] = sum(COPIES[n] for n in FIRST)
TOTAL_COPIES = sum(COPIES.values())


def kernel(
    r_ref, t_ref, b_hbm, space_ref, time_ref, out_ref,
    b, part, part_out, part_in, coef, y_own, y_out, y_in, z_out, z_in, scaled,
    core_out, core_in, own, x_out, x_in, h_own, h_out, h_in, syn, time_columns,
    send_sem, recv_sem, b_sem,
):
    srow, scol, hour = lax.axis_index("srow"), lax.axis_index("scol"), lax.axis_index("hour")
    low, y = srow // Y, srow % Y
    x, core = scol // 2, scol % 2
    width = b.shape[2]
    sites = r_ref.shape[0]
    piece = sites // HOURS

    def hour_peer(o):
        return (srow, scol, (hour + o) % HOURS)

    def x_peer(o):
        return (srow, ((x + o) % X) * 2 + core, hour)

    def y_peer(o):
        return (low * Y + (y + o) % Y, scol, hour)

    core_peer = (srow, x * 2 + (1 - core), hour)
    low_peer = ((1 - low) * Y + y, scol, hour)

    started = {}

    def send(name, i, q, src, dst, peer):
        at = FIRST[name] + i
        copy = pltpu.make_async_remote_copy(
            src_ref=src, dst_ref=dst, send_sem=send_sem.at[q, at], recv_sem=recv_sem.at[q, at],
            device_id=peer, device_id_type=MESH,
        )
        copy.start()
        started[name, i, q] = copy

    def arrived(name, i, q):
        started[name, i, q].wait_recv()

    def group(c):
        return pl.ds(pl.multiple_of(c * sites, sites), sites)

    barrier = pltpu.get_barrier_semaphore()
    peers = [f(o) for f in (hour_peer, x_peer, y_peer) for o in (1, 2, 3)] + [core_peer, low_peer]
    for peer in peers:
        pl.semaphore_signal(barrier, inc=1, device_id=peer, device_id_type=MESH)
    for j in range(b.shape[0]):
        pltpu.make_async_copy(b_hbm.at[:, pl.ds(j * width, width)], b.at[j], b_sem.at[j]).start()

    for i in range(0, time_columns.shape[0], LANES):
        time_columns[i : i + LANES, :] = jnp.broadcast_to(time_ref[:, i : i + LANES], (LANES, LANES)).T

    def project(q):
        value = lax.dot_general(
            t_ref[:, SLICES[q][0] : sum(SLICES[q])], r_ref[...], (((0,), (1,)), ((), ())), preferred_element_type=F32
        )
        for i in range(HOURS):
            block = value[:, i * piece : (i + 1) * piece]
            part[q][i] = block
            part_out[q][i] = block.astype(BF16)
        if q == ORDER[0][1]:
            pl.semaphore_wait(barrier, len(peers))
        for o in (2, 1, 3):
            send("hour_sum", o - 1, q, part_out[q].at[(hour + o) % HOURS], part_in[q].at[o - 1], hour_peer(o))

    def sum_hours(q):
        total = part[q][hour]
        for o in (1, 3, 2):
            arrived("hour_sum", o - 1, q)
            total += part_in[q][o - 1].astype(F32)
        mine = scol * HOURS + hour
        coef[q][mine] = total.astype(BF16)
        for o in (2, 1, 3):
            send("hour_gather", o - 1, q, coef[q].at[mine], coef[q].at[mine], hour_peer(o))

    def gather_x(q):
        for o in (1, 3, 2):
            arrived("hour_gather", o - 1, q)
        mine = coef[q].at[pl.ds(scol * HOURS, HOURS)]
        for o in (2, 1, 3):
            send("x_gather", o - 1, q, mine, mine, x_peer(o))
        send("core_gather", 0, q, mine, mine, core_peer)

    def half(q, j, of_core):
        total = None
        for i in range(X):
            c = i * 2 + of_core
            left = jnp.concatenate([coef[q][c * HOURS + n] for n in range(HOURS)], axis=1)
            term = jnp.dot(left, b[j, group(c), :], preferred_element_type=F32)
            total = term if total is None else total + term
        return total

    def analyse(q):
        for o in (1, 3, 2):
            arrived("x_gather", o - 1, q)
            c = ((x + X - o) % X) * 2 + core
            other = coef[q].at[pl.ds(c * HOURS, HOURS)]
            send("core_gather", o, q, other, other, core_peer)
        if (3, q) == next(o for o in ORDER if o[0] == 3):
            for j in range(b.shape[0]):
                pltpu.make_async_copy(b_hbm.at[:, pl.ds(j * width, width)], b.at[j], b_sem.at[j]).wait()

        def first(j, carry):
            y_own[q][j] = half(q, j, core)
            return carry

        lax.fori_loop(0, Y, first, 0)
        for i in range(4):
            arrived("core_gather", i, q)

        def second(j, carry):
            total = y_own[q][j] + half(q, j, 1 - core)
            y_own[q][j] = total
            y_out[q][j] = total.astype(BF16)
            return carry

        lax.fori_loop(0, Y, second, 0)
        for o in (2, 1, 3):
            send("y_sum", o - 1, q, y_out[q].at[(y + o) % Y], y_in[q].at[o - 1], y_peer(o))

    def sum_y(q):
        total = y_own[q][y]
        for o in (1, 3, 2):
            arrived("y_sum", o - 1, q)
            total += y_in[q][o - 1].astype(F32)
        y_own[q][y] = total
        z_out[q][...] = total.astype(BF16)
        send("z_sum", 0, q, z_out[q], z_in[q], low_peer)

    def scale(q):
        time = time_columns[SLICES[q][0] : sum(SLICES[q]), :]
        product = jnp.concatenate([time] * (width // LANES), axis=1) * space_ref[y]
        ratio = product / (product + noise_level)
        arrived("z_sum", 0, q)
        total = y_own[q][y] + z_in[q][...].astype(F32)
        scaled[q][y] = (total * ratio).astype(BF16)
        for o in (2, 1, 3):
            send("y_gather", o - 1, q, scaled[q].at[y], scaled[q].at[y], y_peer(o))

    def synthesise(q):
        for o in (1, 3, 2):
            arrived("y_gather", o - 1, q)

        def term(c):
            total = None
            for j in range(Y):
                one = lax.dot_general(
                    scaled[q][j], b[j, group(c), :], (((1,), (1,)), ((), ())), preferred_element_type=F32
                )
                total = one if total is None else total + one
            return total

        for o in (2, 1, 3, 0):
            to = (x + o) % X
            core_out[q][to] = term(to * 2 + (1 - core))
            send("core_sum", o, q, core_out[q].at[to], core_in[q].at[to], core_peer)
        for o in (2, 1, 3, 0):
            to = (x + o) % X
            value = term(to * 2 + core)
            arrived("core_sum", o, q)
            value += core_in[q][to]
            if o:
                x_out[q][to] = value.astype(BF16)
                send("x_sum", o - 1, q, x_out[q].at[to], x_in[q].at[o - 1], x_peer(o))
            else:
                own[q][...] = value

    def sum_x(q):
        total = own[q][...]
        for o in (1, 3, 2):
            arrived("x_sum", o - 1, q)
            total += x_in[q][o - 1].astype(F32)
        for i in range(HOURS):
            block = total[:, i * piece : (i + 1) * piece]
            h_own[q][i] = block
            h_out[q][i] = block.astype(BF16)
        for o in (2, 1, 3):
            send("last_sum", o - 1, q, h_out[q].at[(hour + o) % HOURS], h_in[q].at[o - 1], hour_peer(o))

    def sum_last(q):
        total = h_own[q][hour]
        for o in (1, 3, 2):
            arrived("last_sum", o - 1, q)
            total += h_in[q][o - 1].astype(F32)
        mine = syn.at[hour, pl.ds(*SLICES[q])]
        mine[...] = total.astype(BF16)
        for o in (2, 1, 3):
            send("last_gather", o - 1, q, mine, mine, hour_peer(o))

    def finish(q):
        for o in (1, 3, 2):
            arrived("last_gather", o - 1, q)

    stages = [project, sum_hours, gather_x, analyse, sum_y, scale, synthesise, sum_x, sum_last, finish]
    for at, q in ORDER:
        stages[at](q)

    out_ref[...] = syn[...]
    for copy in started.values():
        copy.wait_send()


def on_device(readings, space_basis, time_modes, space_power, time_power):
    sites, hours = readings.shape
    rows, columns = space_basis.shape
    every_mode = time_modes.shape[1]
    piece, width = sites // HOURS, columns // Y
    groups = rows // sites

    def chunked(dtype, *shape):
        return [pltpu.VMEM((*shape[:-1], modes, shape[-1]), dtype) for _, modes in SLICES]

    in_vmem = pl.BlockSpec(memory_space=pltpu.VMEM)
    synthesis = pl.pallas_call(
        kernel,
        out_shape=jax.ShapeDtypeStruct((HOURS, every_mode, piece), BF16),
        in_specs=[in_vmem, in_vmem, pl.BlockSpec(memory_space=pl.ANY), in_vmem, in_vmem],
        out_specs=in_vmem,
        scratch_shapes=[
            pltpu.VMEM((Y, rows, width), BF16),
            chunked(F32, HOURS, piece),
            chunked(BF16, HOURS, piece),
            chunked(BF16, 3, piece),
            chunked(BF16, groups * HOURS, piece),
            chunked(F32, Y, width),
            chunked(BF16, Y, width),
            chunked(BF16, 3, width),
            chunked(BF16, width),
            chunked(BF16, width),
            chunked(BF16, Y, width),
            chunked(F32, X, sites),
            chunked(F32, X, sites),
            chunked(F32, sites),
            chunked(BF16, X, sites),
            chunked(BF16, 3, sites),
            chunked(F32, HOURS, piece),
            chunked(BF16, HOURS, piece),
            chunked(BF16, 3, piece),
            pltpu.VMEM((HOURS, every_mode, piece), BF16),
            pltpu.VMEM((every_mode, LANES), F32),
            pltpu.SemaphoreType.DMA((CHUNKS, TOTAL_COPIES)),
            pltpu.SemaphoreType.DMA((CHUNKS, TOTAL_COPIES)),
            pltpu.SemaphoreType.DMA((Y,)),
        ],
        compiler_params=pltpu.CompilerParams(
            collective_id=0, has_side_effects=True, vmem_limit_bytes=58 * 2**20
        ),
        name="transform",
    )(readings, time_modes, space_basis, space_power.reshape(Y, 1, width), time_power.reshape(1, every_mode))
    posterior = jnp.einsum('hms,tm->hst', synthesis, time_modes, preferred_element_type=F32)
    return posterior.reshape(sites, hours).astype(BF16)


def solution(mesh):
    return jax.shard_map(
        on_device,
        mesh=mesh,
        in_specs=(
            P(("srow", "scol"), "hour"),
            P("srow", ("scol", "hour")),
            P("hour", None),
            P(("scol", "hour")),
            P(),
        ),
        out_specs=P(("srow", "scol"), "hour"),
        check_vma=False,
    )
```

time: 118 us -> 102 us (0.86)
  Pallas kernels: 113 us -> 98.8 us
  local copies, waits for them, and re-layouts: 3.91 us -> 0.01 us
  matrix products: 0 us -> 2.95 us
    pallas_call x1, Pallas kernels: 113 us -> 98.8 us  [on_device(): pl.pallas_call(kernel, out_shape=jax.ShapeDtypeStruct((HOURS, every_mode,...]
    dot_general x0 -> x1, matrix products: none -> 2.95 us  [on_device(): jnp.einsum('hms,tm->hst', synthesis, time_modes, preferred_element_type=F32)]
    unnamed x1 -> x2, local copies, waits for them, and re-layouts: 2.37 us -> 0.01 us
    reshape x1 -> x0, local copies, waits for them, and re-layouts: 1.53 us -> none  [on_device(): time_power.reshape(every_mode, 1)]
where the time goes in v2:
time: 102 us
  Pallas kernels  98.8 us (97%)
  matrix products  2.95 us (3%)
    pallas_call x1, Pallas kernels, on_device(): pl.pallas_call(kernel, out_shape=jax.ShapeDtypeStruct((HOURS, every_mode,...  98.8 us
    dot_general x1, matrix products, on_device(): jnp.einsum('hms,tm->hst', synthesis, time_modes, preferred_element_type=F32)  2.95 us

profile of v2, /device:TPU:9, one launch (start us, length us, event | category | flops | bytes accessed | tf_op | source)
XLA Modules:
  0.0 101.8 jit_solution(7871370387820465759)
XLA Ops:
  0.0 0.0 copy-start
  0.0 98.8 %transform.1 = bf16[4,512,128]{2,1,0:T(8,128)(2,1)} custom-call(bf16[512,1152]{1,0:T(8,128)(2,1)} %r_ref.1, bf16[1152,512]{1,0:T(8,128)(2,1)} %t_ref.1, bf16[4096,1024]{1,0:T(8,128)(2,1)} %b_hbm.1, f32[4,1,256]{2,1,0:T(1,128)} %bitcast.7, f32[1,512]{1,0:T(1,128)} %bitcast.8), custom_call_target="tpu_custom_call" | custom-call | tf_op jit(solution)/shard_map/transform/pallas_call | solution.py:245
  98.8 0.0 copy-done
  98.8 2.9 %convolution_convert_fusion = bf16[4,128,1152]{2,1,0:T(8,128)(2,1)} fusion(bf16[4,512,128]{2,1,0:T(8,128)(2,1)} %transform.1, bf16[1152,512]{1,0:T(8,128)(2,1)S(1)} %copy-done), kind=kOutput, calls=%fused_computation | convolution fusion | flops 604569600 | bytes 2883584 | tf_op jit(solution)/shard_map/hms,tm->hst/dot_general | solution.py:281
Async XLA Ops:
  0.0 98.8 %copy-start = (bf16[1152,512]{1,0:T(8,128)(2,1)S(1)}, bf16[1152,512]{1,0:T(8,128)(2,1)}, u32[]{:S(2)}) copy-start(bf16[1152,512]{1,0:T(8,128)(2,1)} %t_ref.1) | copy-start | bytes 3538948

commit v3 on v2

--- a/solution.py
+++ b/solution.py
@@ -17,9 +17,9 @@
 X, Y, HOURS = 4, 4, 4
 
 ORDER = (
-    (0, 3), (0, 0), (0, 1), (1, 3), (1, 1), (0, 2), (2, 3), (1, 2), (2, 1), (3, 3), (2, 2), (1, 0), (3, 1), (4, 3),
-    (2, 0), (5, 3), (4, 1), (3, 2), (5, 1), (6, 3), (3, 0), (4, 2), (6, 1), (5, 2), (4, 0), (7, 3), (5, 0), (6, 2),
-    (7, 1), (6, 0), (8, 3), (8, 1), (7, 2), (7, 0), (8, 2), (8, 0), (9, 3), (9, 1), (9, 0), (9, 2),
+    (0, 1), (0, 3), (0, 0), (1, 1), (1, 0), (0, 2), (2, 1), (1, 3), (2, 0), (1, 2), (3, 1), (2, 2), (3, 0), (4, 1),
+    (2, 3), (5, 1), (4, 0), (3, 2), (5, 0), (6, 1), (3, 3), (4, 2), (6, 0), (5, 2), (4, 3), (7, 1), (5, 3), (6, 2),
+    (7, 0), (6, 3), (8, 1), (8, 0), (7, 2), (9, 1), (7, 3), (8, 2), (9, 0), (8, 3), (9, 3), (9, 2),
 )
 
 COPIES = dict(hour_sum=3, hour_gather=3, x_gather=3, core_gather=4, y_sum=3, z_sum=1, y_gather=3, core_sum=4, x_sum=3, last_sum=3, last_gather=3)
@@ -30,10 +30,10 @@
 
 
 def kernel(
-    r_ref, t_ref, b_hbm, space_ref, time_ref, out_ref,
+    r_ref, t_ref, b_hbm, space_ref, time_ref, out_hbm,
     b, part, part_out, part_in, coef, y_own, y_out, y_in, z_out, z_in, scaled,
     core_out, core_in, own, x_out, x_in, h_own, h_out, h_in, syn, time_columns,
-    send_sem, recv_sem, b_sem,
+    send_sem, recv_sem, b_sem, out_sem,
 ):
     srow, scol, hour = lax.axis_index("srow"), lax.axis_index("scol"), lax.axis_index("hour")
     low, y = srow // Y, srow % Y
@@ -183,13 +183,13 @@
 
         for o in (2, 1, 3, 0):
             to = (x + o) % X
-            core_out[q][to] = term(to * 2 + (1 - core))
+            core_out[q][to] = term(to * 2 + (1 - core)).astype(BF16)
             send("core_sum", o, q, core_out[q].at[to], core_in[q].at[to], core_peer)
         for o in (2, 1, 3, 0):
             to = (x + o) % X
             value = term(to * 2 + core)
             arrived("core_sum", o, q)
-            value += core_in[q][to]
+            value += core_in[q][to].astype(F32)
             if o:
                 x_out[q][to] = value.astype(BF16)
                 send("x_sum", o - 1, q, x_out[q].at[to], x_in[q].at[o - 1], x_peer(o))
@@ -221,14 +221,20 @@
     def finish(q):
         for o in (1, 3, 2):
             arrived("last_gather", o - 1, q)
+        done = syn.at[:, pl.ds(*SLICES[q])]
+        stored.append(pltpu.make_async_copy(done, out_hbm.at[:, pl.ds(*SLICES[q])], out_sem.at[q]))
+        stored[-1].start()
+
+    stored = []
 
     stages = [project, sum_hours, gather_x, analyse, sum_y, scale, synthesise, sum_x, sum_last, finish]
     for at, q in ORDER:
         stages[at](q)
 
-    out_ref[...] = syn[...]
     for copy in started.values():
         copy.wait_send()
+    for copy in stored:
+        copy.wait()
 
 
 def on_device(readings, space_basis, time_modes, space_power, time_power):
@@ -246,7 +252,7 @@
         kernel,
         out_shape=jax.ShapeDtypeStruct((HOURS, every_mode, piece), BF16),
         in_specs=[in_vmem, in_vmem, pl.BlockSpec(memory_space=pl.ANY), in_vmem, in_vmem],
-        out_specs=in_vmem,
+        out_specs=pl.BlockSpec(memory_space=pl.ANY),
         scratch_shapes=[
             pltpu.VMEM((Y, rows, width), BF16),
             chunked(F32, HOURS, piece),
@@ -259,8 +265,8 @@
             chunked(BF16, width),
             chunked(BF16, width),
             chunked(BF16, Y, width),
-            chunked(F32, X, sites),
-            chunked(F32, X, sites),
+            chunked(BF16, X, sites),
+            chunked(BF16, X, sites),
             chunked(F32, sites),
             chunked(BF16, X, sites),
             chunked(BF16, 3, sites),
@@ -272,6 +278,7 @@
             pltpu.SemaphoreType.DMA((CHUNKS, TOTAL_COPIES)),
             pltpu.SemaphoreType.DMA((CHUNKS, TOTAL_COPIES)),
             pltpu.SemaphoreType.DMA((Y,)),
+            pltpu.SemaphoreType.DMA((CHUNKS,)),
         ],
         compiler_params=pltpu.CompilerParams(
             collective_id=0, has_side_effects=True, vmem_limit_bytes=58 * 2**20

time: 102 us -> 102 us (level)
  no operation moved by 1% of the time
where the time goes in v3:
time: 102 us
  Pallas kernels  98.5 us (97%)
  matrix products  2.95 us (3%)
    pallas_call x1, Pallas kernels, on_device(): pl.pallas_call(kernel, out_shape=jax.ShapeDtypeStruct((HOURS, every_mode,...  98.5 us
    dot_general x1, matrix products, on_device(): jnp.einsum('hms,tm->hst', synthesis, time_modes, preferred_element_type=F32)  2.95 us

profile of v3, /device:TPU:9, one launch (start us, length us, event | category | flops | bytes accessed | tf_op | source)
XLA Modules:
  0.0 101.5 jit_solution(5004169778541317864)
XLA Ops:
  0.0 0.0 copy-start
  0.0 98.5 %transform.1 = bf16[4,512,128]{2,1,0:T(8,128)(2,1)} custom-call(bf16[512,1152]{1,0:T(8,128)(2,1)} %r_ref.1, bf16[1152,512]{1,0:T(8,128)(2,1)} %t_ref.1, bf16[4096,1024]{1,0:T(8,128)(2,1)} %b_hbm.1, f32[4,1,256]{2,1,0:T(1,128)} %bitcast.7, f32[1,512]{1,0:T(1,128)} %bitcast.8), custom_call_target="tpu_custom_call" | custom-call | tf_op jit(solution)/shard_map/transform/pallas_call | solution.py:251
  98.6 0.0 copy-done
  98.6 2.9 %convolution_convert_fusion = bf16[4,128,1152]{2,1,0:T(8,128)(2,1)} fusion(bf16[4,512,128]{2,1,0:T(8,128)(2,1)} %transform.1, bf16[1152,512]{1,0:T(8,128)(2,1)S(1)} %copy-done), kind=kOutput, calls=%fused_computation | convolution fusion | flops 604569600 | bytes 2883584 | tf_op jit(solution)/shard_map/hms,tm->hst/dot_general | solution.py:288
Async XLA Ops:
  0.0 98.6 %copy-start = (bf16[1152,512]{1,0:T(8,128)(2,1)S(1)}, bf16[1152,512]{1,0:T(8,128)(2,1)}, u32[]{:S(2)}) copy-start(bf16[1152,512]{1,0:T(8,128)(2,1)} %t_ref.1) | copy-start | bytes 3538948
